TPU v7x, 32 devices: a whole 2x2x4 slice. The times are simulated.
32 devices in a mesh: outer: 8 (over z, x), inner: 4 (over y, core).
Axes of the slice: x: 2, y: 2, z: 4, core: 2. Of those that a mesh axis runs over, the one named last changes fastest.
Arguments:
- queries: bfloat16 [4096, 128], P('inner'), may hold values from -150 to 150
- key_rows: bfloat16 [8192, 128], P(('outer', 'inner')), may hold values from -4.5 to 4.5
- value_rows: bfloat16 [8192, 128], P(('outer', 'inner')), may hold values from -6 to 6
Outputs:
- attended: bfloat16 [4096, 128], P('inner')
All inputs are finite; a program needn't handle non-finite values.
Results may differ from a plain program's by a relative error of at most 0.015.
Values may be sent and summed in bfloat16 or wider, within the bound.
A program may use at most 64 MiB of HBM per device.

v0:
```python
import math

import jax
import jax.numpy as jnp
from jax import lax
from jax.sharding import PartitionSpec as P


def merged(part, axis, combine):
    gathered = jax.tree.map(lambda a: lax.all_gather(a, axis), part)

    def take(source):
        return jax.tree.map(lambda a: lax.dynamic_index_in_dim(a, source, 0, False), gathered)

    return lax.fori_loop(
        1, lax.axis_size(axis), lambda source, state: combine(state, take(source)), take(0)
    )


def combine_partial(left, right):
    left_sum, left_peak, left_total = left
    right_sum, right_peak, right_total = right
    joint_peak = jnp.maximum(left_peak, right_peak)
    left_factor = jnp.exp(left_peak - joint_peak)
    right_factor = jnp.exp(right_peak - joint_peak)
    joint_sum = left_sum * left_factor[:, None] + right_sum * right_factor[:, None]
    joint_total = left_total * left_factor + right_total * right_factor
    return (joint_sum, joint_peak, joint_total)


def on_device(queries, key_rows, value_rows):
    query_count, head_size = queries.shape
    score_scale = 1.0 / math.sqrt(head_size)

    def advance(running, tiles):
        weighted, row_peak, row_total = running
        key_tile, value_tile = tiles
        scores = (
            lax.dot_general(
                queries, key_tile, (((1,), (1,)), ((), ())), preferred_element_type=jnp.float32
            )
            * score_scale
        )
        new_peak = jnp.maximum(row_peak, jnp.max(scores, axis=1))
        rescale = jnp.exp(row_peak - new_peak)
        probs = jnp.exp(scores - new_peak[:, None])
        new_total = row_total * rescale + jnp.sum(probs, axis=1)
        new_weighted = weighted * rescale[:, None] + jnp.dot(
            probs.astype(jnp.bfloat16), value_tile, preferred_element_type=jnp.float32
        )
        return ((new_weighted, new_peak, new_total), None)

    start_state = (
        jnp.zeros((query_count, head_size), jnp.float32),
        jnp.full((query_count,), -1e30, jnp.float32),
        jnp.zeros((query_count,), jnp.float32),
    )
    key_part = lax.all_gather(key_rows, "inner", axis=0, tiled=True)
    value_part = lax.all_gather(value_rows, "inner", axis=0, tiled=True)
    row_count = key_part.shape[0]
    block_rows = math.gcd(row_count, 256)
    key_tiles = key_part.reshape(row_count // block_rows, block_rows, head_size)
    value_tiles = value_part.reshape(row_count // block_rows, block_rows, head_size)
    result, unused = lax.scan(advance, start_state, (key_tiles, value_tiles))
    weighted, row_peak, row_total = result
    joint_sum, joint_peak, joint_total = merged(
        (weighted, row_peak, row_total), "outer", combine_partial
    )
    attended = (joint_sum / joint_total[:, None]).astype(jnp.bfloat16)
    return attended


def solution(mesh):
    return jax.shard_map(
        on_device,
        mesh=mesh,
        in_specs=(P("inner", None), P(("outer", "inner"), None), P(("outer", "inner"), None)),
        out_specs=P("inner", None),
        check_vma=False,
    )
```

profile of v0, /device:TPU:0, one launch (start us, length us, event | category | flops | bytes accessed | tf_op | source)
XLA Modules:
  0.0 124.2 jit_solution(15612764472093649412)
XLA Ops:
  6.5 0.0 all-gather.5.cloned.1.call-start
  6.5 7.4 %all_gather.24 = bf16[1024,128]{1,0:T(8,128)(2,1)S(1)} all-gather(bf16[256,128]{1,0:T(8,128)(2,1)} %param.8), channel_id=1, replica_groups=mesh['outer'=8,'inner'=4] {'inner'}, dimensions={0}, use_global_device_ids=true | all-gather | bytes 327680 | tf_op jit(solution)/shard_map/all_gather | solution.py:58
  14.0 6.1 %all_gather.25 = bf16[1024,128]{1,0:T(8,128)(2,1)S(1)} all-gather(bf16[256,128]{1,0:T(8,128)(2,1)} %param.9), channel_id=1, replica_groups=mesh['outer'=8,'inner'=4] {'inner'}, dimensions={0}, use_global_device_ids=true | all-gather | bytes 327680 | tf_op jit(solution)/shard_map/all_gather | solution.py:59
  20.0 8.0 %while.35 = (s32[]{:T(128)}, f32[1024,128]{1,0:T(8,128)S(1)}, f32[1024]{0:T(1024)S(1)}, f32[1024]{0:T(1024)S(1)}, bf16[4,256,128]{2,1,0:T(8,128)(2,1)S(1)}, /*in...) while((s32[]{:T(128)}, f32[1024,128]{1,0:T(8,128)S(1)}, ...), condition=%wide.region_3.4_spmd.clone, body=%wide.region_0.3_spmd.clone.sunk | while | flops 136188928 | bytes 4653177 | solution.py:64
  20.0 1.3 %fusion.25 = (f32[1024]{0:T(1024)S(1)}, f32[256,1024]{1,0:T(8,128)S(1)}) fusion(bf16[1024,128]{1,0:T(8,128)(2,1)} %get-tuple-element.417, bf16[4,256,128]{2,1,0:T(8,128)(2,1)S(1)} %get-tuple-element.416, s32[]{:T(128)S(6)} %copy.8), kind=kOutput, calls=%fused_computation.25.clone.1 | convolution fusion | flops 67632128 | bytes 1380356 | tf_op jit(solution)/shard_map/while/body/eval_jaxpr/dot_general | solution.py:39
  21.3 0.2 fusion.26
  21.5 0.5 convolution_add_fusion.2
  22.0 1.3 %fusion.25 = (f32[1024]{0:T(1024)S(1)}, f32[256,1024]{1,0:T(8,128)S(1)}) fusion(bf16[1024,128]{1,0:T(8,128)(2,1)} %get-tuple-element.417, bf16[4,256,128]{2,1,0:T(8,128)(2,1)S(1)} %get-tuple-element.416, s32[]{:T(128)S(6)} %copy.8), kind=kOutput, calls=%fused_computation.25.clone.1 | convolution fusion | flops 67632128 | bytes 1380356 | tf_op jit(solution)/shard_map/while/body/eval_jaxpr/dot_general | solution.py:39
  23.3 0.2 fusion.26
  23.5 0.5 convolution_add_fusion.2
  24.0 1.3 %fusion.25 = (f32[1024]{0:T(1024)S(1)}, f32[256,1024]{1,0:T(8,128)S(1)}) fusion(bf16[1024,128]{1,0:T(8,128)(2,1)} %get-tuple-element.417, bf16[4,256,128]{2,1,0:T(8,128)(2,1)S(1)} %get-tuple-element.416, s32[]{:T(128)S(6)} %copy.8), kind=kOutput, calls=%fused_computation.25.clone.1 | convolution fusion | flops 67632128 | bytes 1380356 | tf_op jit(solution)/shard_map/while/body/eval_jaxpr/dot_general | solution.py:39
  25.3 0.2 fusion.26
  25.5 0.5 convolution_add_fusion.2
  26.1 1.3 %fusion.25 = (f32[1024]{0:T(1024)S(1)}, f32[256,1024]{1,0:T(8,128)S(1)}) fusion(bf16[1024,128]{1,0:T(8,128)(2,1)} %get-tuple-element.417, bf16[4,256,128]{2,1,0:T(8,128)(2,1)S(1)} %get-tuple-element.416, s32[]{:T(128)S(6)} %copy.8), kind=kOutput, calls=%fused_computation.25.clone.1 | convolution fusion | flops 67632128 | bytes 1380356 | tf_op jit(solution)/shard_map/while/body/eval_jaxpr/dot_general | solution.py:39
  27.3 0.2 fusion.26
  27.5 0.5 convolution_add_fusion.2
  28.1 0.0 copy-start
  28.1 0.8 copy-done
  28.9 0.0 all-gather.5.cloned.1.call-update
  28.9 31.1 %all-gather.2 = f32[8192]{0:T(1024)S(1)} all-gather(f32[1024]{0:T(1024)S(1)} %get-tuple-element.223), channel_id=4, replica_groups=mesh['outer'=8,'inner'=4] {'outer'}, dimensions={0}, use_global_device_ids=true | all-gather | bytes 36864 | tf_op jit(solution)/shard_map/all_gather | solution.py:10
  60.0 31.1 %all-gather.1 = f32[8192]{0:T(1024)S(1)} all-gather(f32[1024]{0:T(1024)S(1)} %get-tuple-element.222), channel_id=3, replica_groups=mesh['outer'=8,'inner'=4] {'outer'}, dimensions={0}, use_global_device_ids=true | all-gather | bytes 36864 | tf_op jit(solution)/shard_map/all_gather | solution.py:10
  91.1 13.3 %all-gather.5.cloned.1.call-done = f32[8192,128]{1,0:T(8,128)} async-done(((f32[1024,128]{1,0:T(8,128)}), f32[8192,128]{1,0:T(8,128)}) %all-gather.5.cloned.1.call-update) | async-done | bytes 4194320 | tf_op jit(solution)/shard_map/all_gather | solution.py:10
  104.4 1.1 slice.6
  105.5 10.9 %while.34 = (s32[]{:T(128)}, f32[1024,128]{1,0:T(8,128)S(1)}, f32[1024]{0:T(1024)S(1)}, f32[1024]{0:T(1024)S(1)}, f32[8,1024]{1,0:T(8,128)S(1)}, /*index=5*/f32[...) while((s32[]{:T(128)}, f32[1024,128]{1,0:T(8,128)S(1)}, ...), condition=%wide.region_5.6_spmd, body=%wide.region_4.5_spmd.sunk | while | flops 399365 | bytes 1630351 | solution.py:15
  105.6 1.5 %fusion.21 = f32[1024,128]{1,0:T(8,128)S(1)} fusion(f32[8,1024,128]{2,1,0:T(8,128)} %get-tuple-element.446, s32[]{:T(128)S(6)} %select_n.18, f32[1024,128]{1,0:T(8,128)S(1)} %get-tuple-element.432, f32[1024]{0:T(1024)S(1)} %get-tuple-element.379, f32[1024]{0:T(1024)S(1)} %get-tuple-element.380), kind=kLoop, calls=%fused_computation.1.clone.1 | loop fusion | flops 393216 | bytes 1581060 | tf_op jit(solution)/shard_map/while/body/eval_jaxpr/add | solution.py:26
  107.1 1.5 %fusion.21 = f32[1024,128]{1,0:T(8,128)S(1)} fusion(f32[8,1024,128]{2,1,0:T(8,128)} %get-tuple-element.446, s32[]{:T(128)S(6)} %select_n.18, f32[1024,128]{1,0:T(8,128)S(1)} %get-tuple-element.432, f32[1024]{0:T(1024)S(1)} %get-tuple-element.379, f32[1024]{0:T(1024)S(1)} %get-tuple-element.380), kind=kLoop, calls=%fused_computation.1.clone.1 | loop fusion | flops 393216 | bytes 1581060 | tf_op jit(solution)/shard_map/while/body/eval_jaxpr/add | solution.py:26
  108.7 1.5 %fusion.21 = f32[1024,128]{1,0:T(8,128)S(1)} fusion(f32[8,1024,128]{2,1,0:T(8,128)} %get-tuple-element.446, s32[]{:T(128)S(6)} %select_n.18, f32[1024,128]{1,0:T(8,128)S(1)} %get-tuple-element.432, f32[1024]{0:T(1024)S(1)} %get-tuple-element.379, f32[1024]{0:T(1024)S(1)} %get-tuple-element.380), kind=kLoop, calls=%fused_computation.1.clone.1 | loop fusion | flops 393216 | bytes 1581060 | tf_op jit(solution)/shard_map/while/body/eval_jaxpr/add | solution.py:26
  110.2 1.5 %fusion.21 = f32[1024,128]{1,0:T(8,128)S(1)} fusion(f32[8,1024,128]{2,1,0:T(8,128)} %get-tuple-element.446, s32[]{:T(128)S(6)} %select_n.18, f32[1024,128]{1,0:T(8,128)S(1)} %get-tuple-element.432, f32[1024]{0:T(1024)S(1)} %get-tuple-element.379, f32[1024]{0:T(1024)S(1)} %get-tuple-element.380), kind=kLoop, calls=%fused_computation.1.clone.1 | loop fusion | flops 393216 | bytes 1581060 | tf_op jit(solution)/shard_map/while/body/eval_jaxpr/add | solution.py:26
  111.8 1.5 %fusion.21 = f32[1024,128]{1,0:T(8,128)S(1)} fusion(f32[8,1024,128]{2,1,0:T(8,128)} %get-tuple-element.446, s32[]{:T(128)S(6)} %select_n.18, f32[1024,128]{1,0:T(8,128)S(1)} %get-tuple-element.432, f32[1024]{0:T(1024)S(1)} %get-tuple-element.379, f32[1024]{0:T(1024)S(1)} %get-tuple-element.380), kind=kLoop, calls=%fused_computation.1.clone.1 | loop fusion | flops 393216 | bytes 1581060 | tf_op jit(solution)/shard_map/while/body/eval_jaxpr/add | solution.py:26
  113.4 1.5 %fusion.21 = f32[1024,128]{1,0:T(8,128)S(1)} fusion(f32[8,1024,128]{2,1,0:T(8,128)} %get-tuple-element.446, s32[]{:T(128)S(6)} %select_n.18, f32[1024,128]{1,0:T(8,128)S(1)} %get-tuple-element.432, f32[1024]{0:T(1024)S(1)} %get-tuple-element.379, f32[1024]{0:T(1024)S(1)} %get-tuple-element.380), kind=kLoop, calls=%fused_computation.1.clone.1 | loop fusion | flops 393216 | bytes 1581060 | tf_op jit(solution)/shard_map/while/body/eval_jaxpr/add | solution.py:26
  114.9 1.5 %fusion.21 = f32[1024,128]{1,0:T(8,128)S(1)} fusion(f32[8,1024,128]{2,1,0:T(8,128)} %get-tuple-element.446, s32[]{:T(128)S(6)} %select_n.18, f32[1024,128]{1,0:T(8,128)S(1)} %get-tuple-element.432, f32[1024]{0:T(1024)S(1)} %get-tuple-element.379, f32[1024]{0:T(1024)S(1)} %get-tuple-element.380), kind=kLoop, calls=%fused_computation.1.clone.1 | loop fusion | flops 393216 | bytes 1581060 | tf_op jit(solution)/shard_map/while/body/eval_jaxpr/add | solution.py:26
  116.4 0.9 divide_convert_fusion
  (33 shorter events, 0.3 us)
Async XLA Ops:
  6.5 97.9 %all-gather.5.cloned.1.call-start = ((), (), s32[]{:S(2)}) async-start(), calls=%async_computation | async-start | bytes 4718592 | tf_op jit(solution)/shard_map/all_gather | solution.py:10
  28.1 0.8 copy-start
Sparse Core Ops, SparseCore 0:
  29.0 75.3 all-gather.4
where the time goes:
time: 125 us; the launch traced here: 124 us
  blocking collectives  75.7 us (61%)
  between operations  13.4 us (11%)
  waiting for transfers between devices  13.3 us (11%)
  other arithmetic  12.3 us (10%)
  matrix products  7.08 us (6%)
  local copies, waits for them, and re-layouts  2.01 us (2%)
    all_gather x2, blocking collectives, merged(): gathered = jax.tree.map(lambda a: lax.all_gather(a, axis), part)  62.2 us
    all_gather x1, waiting for transfers between devices, merged(): gathered = jax.tree.map(lambda a: lax.all_gather(a, axis), part)  13.3 us
    add x7, other arithmetic, combine_partial(): left_sum * left_factor[:, None] + right_sum * right_factor[:, None]  10.5 us
    all_gather x1, blocking collectives, on_device(): key_part = lax.all_gather(key_rows, 'inner', axis=0, tiled=True)  7.42 us
    all_gather x1, blocking collectives, on_device(): value_part = lax.all_gather(value_rows, 'inner', axis=0, tiled=True)  6.06 us
    dot_general x4, matrix products, advance(): lax.dot_general(queries, key_tile, (((1,), (1,)), ((), ())), preferred_el...  5.03 us
  transfers between devices with their start and end apart: 1, of which 1 were waited for; matrix products, arithmetic and copies ran while one was open for 0% of the time, Pallas kernels for 0%

commit v1 on v0

v1 whole, which is shorter than its diff:
```python
import functools
import math

import jax
import jax.numpy as jnp
from jax import lax
from jax.experimental import pallas as pl
from jax.experimental.pallas import tpu as pltpu
from jax.sharding import PartitionSpec as P

MESH = pl.DeviceIdType.MESH
K, V = 0, 1


def kernel(outer_size, inner_size, q_hbm, k_hbm, v_hbm, out_ref, q_vm, kv, send_acc, recv_acc,
           send_stat, recv_stat, local_sem, kv_send, kv_recv, z_send, z_recv, g_send, g_recv):
    nz, ny = outer_size // 2, inner_size // 2
    queries, head = out_ref.shape
    half = queries // 2
    rows = half // nz
    outer, inner = lax.axis_index("outer"), lax.axis_index("inner")
    z, x = outer // 2, outer % 2
    y, core = inner // 2, inner % 2

    x_peer = (z * 2 + (1 - x), inner)
    sibling = (outer, y * 2 + (1 - core))

    def y_peer(j):
        return (outer, lax.rem(y + j, ny) * 2 + core)

    def z_peer(j):
        return (lax.rem(z + j, nz) * 2 + x, inner)

    local = [
        pltpu.make_async_copy(k_hbm, kv.at[0, 0, K, 0], local_sem.at[0]),
        pltpu.make_async_copy(q_hbm.at[pl.ds(pl.multiple_of(x * half, half), half)], q_vm, local_sem.at[1]),
        pltpu.make_async_copy(v_hbm, kv.at[0, 0, V, 0], local_sem.at[2]),
    ]
    for copy in local:
        copy.start()

    barrier = pltpu.get_barrier_semaphore()
    peers = [x_peer, sibling] + [y_peer(j) for j in range(1, ny)] + [z_peer(j) for j in range(1, nz)]
    for peer in peers:
        pl.semaphore_signal(barrier, inc=1, device_id=peer, device_id_type=MESH)
    pl.semaphore_wait(barrier, len(peers))

    flying = {}

    def send(src, slot, peer):
        copy = pltpu.make_async_remote_copy(
            src_ref=src,
            dst_ref=kv.at[slot],
            send_sem=kv_send.at[slot],
            recv_sem=kv_recv.at[slot],
            device_id=peer,
            device_id_type=MESH,
        )
        copy.start()
        flying[slot] = copy

    def arrive(*slot):
        flying[slot].wait_recv()

    send(k_hbm, (1, 0, K, 0), x_peer)
    for j in range(1, ny):
        send(v_hbm, (0, ny - j, V, 0), y_peer(j))
    send(k_hbm, (0, 0, K, 1), sibling)
    send(v_hbm, (0, 0, V, 1), sibling)
    send(v_hbm, (1, 0, V, 0), x_peer)
    for j in range(1, ny):
        send(k_hbm, (0, ny - j, K, 0), y_peer(j))

    to_exponent = math.log2(math.e) / math.sqrt(head)

    def advance(state, keys, values):
        scores = lax.dot_general(
            keys, q_vm[...], (((1,), (1,)), ((), ())), preferred_element_type=jnp.float32
        ) * to_exponent
        peak = jnp.max(scores, axis=0, keepdims=True)
        if state is not None:
            peak = jnp.maximum(peak, state[1])
        probs = jnp.exp2(scores - peak)
        total = jnp.sum(probs, axis=0, keepdims=True)
        weighted = lax.dot_general(
            values, probs.astype(jnp.bfloat16), (((0,), (0,)), ((), ())), preferred_element_type=jnp.float32
        )
        if state is not None:
            factor = jnp.exp2(state[1] - peak)
            weighted = weighted + state[0] * factor
            total = total + state[2] * factor
        return weighted, peak, total

    def one(state, xr, yr, c):
        return advance(state, kv[xr, yr, K, c], kv[xr, yr, V, c])

    def chip(state, xr, yr):
        return advance(
            state, kv[xr, yr, K].reshape(-1, head), kv[xr, yr, V].reshape(-1, head)
        )

    for copy in local:
        copy.wait()
    state = one(None, 0, 0, 0)
    arrive(0, 0, K, 1)
    arrive(0, 0, V, 1)
    state = one(state, 0, 0, 1)

    arrive(1, 0, K, 0)
    for j in range(1, ny):
        send(kv.at[1, 0, K, 0], (1, ny - j, K, 0), y_peer(j))
    send(kv.at[1, 0, K, 0], (1, 0, K, 1), sibling)
    for yr in range(ny - 1, 0, -1):
        arrive(0, yr, V, 0)
        send(kv.at[0, yr, V, 0], (1, yr, V, 0), x_peer)
        send(kv.at[0, yr, V, 0], (0, yr, V, 1), sibling)
    arrive(1, 0, V, 0)
    send(kv.at[1, 0, V, 0], (1, 0, V, 1), sibling)
    for yr in range(ny - 1, 0, -1):
        arrive(0, yr, K, 0)
        send(kv.at[0, yr, K, 0], (0, yr, K, 1), sibling)
    arrive(1, 0, K, 1)
    arrive(1, 0, V, 1)
    state = chip(state, 1, 0)
    for yr in range(ny - 1, 0, -1):
        arrive(0, yr, K, 1)
        arrive(0, yr, V, 1)
        state = chip(state, 0, yr)
    for yr in range(ny - 1, 0, -1):
        for which in (K, V):
            arrive(1, yr, which, 0)
            send(kv.at[1, yr, which, 0], (1, yr, which, 1), sibling)
        state = one(state, 1, yr, 0)
    for yr in range(ny - 1, 0, -1):
        for which in (K, V):
            arrive(1, yr, which, 1)
        state = one(state, 1, yr, 1)

    weighted, peak, total = state
    is_peak = lax.broadcasted_iota(jnp.int32, (8, half), 0) < 4
    stat = jnp.where(is_peak, peak, total)
    for zt in range(nz):
        send_acc[zt] = weighted[:, zt * rows:(zt + 1) * rows].astype(jnp.bfloat16)
        send_stat[zt] = stat[:, zt * rows:(zt + 1) * rows]
    parts = []
    for j in range(1, nz):
        target = lax.rem(z + j, nz)
        for at, (src, dst) in enumerate(((send_stat, recv_stat), (send_acc, recv_acc))):
            copy = pltpu.make_async_remote_copy(
                src_ref=src.at[target],
                dst_ref=dst.at[nz - j],
                send_sem=z_send.at[j, at],
                recv_sem=z_recv.at[nz - j, at],
                device_id=z_peer(j),
                device_id_type=MESH,
            )
            copy.start()
            parts.append(copy)
    for copy in parts:
        copy.wait_recv()
    stats = [send_stat[z]] + [recv_stat[s] for s in range(1, nz)]
    sums = [send_acc[z]] + [recv_acc[s] for s in range(1, nz)]
    joint_peak = functools.reduce(jnp.maximum, [s[0:1] for s in stats])
    joint_total = jnp.zeros_like(joint_peak)
    joint_sum = jnp.zeros((head, rows), jnp.float32)
    for s, a in zip(stats, sums):
        factor = jnp.exp2(s[0:1] - joint_peak)
        joint_total = joint_total + s[4:5] * factor
        joint_sum = joint_sum + a.astype(jnp.float32) * factor

    def block(xr, source):
        return out_ref.at[pl.ds(pl.multiple_of((xr * nz + source) * rows, rows), rows)]

    mine = block(x, z)
    mine[...] = (joint_sum / joint_total).T.astype(jnp.bfloat16)

    def share(view, xr, zr, peer):
        copy = pltpu.make_async_remote_copy(
            src_ref=view,
            dst_ref=view,
            send_sem=g_send.at[xr, zr],
            recv_sem=g_recv.at[xr, zr],
            device_id=peer,
            device_id_type=MESH,
        )
        copy.start()
        return copy

    across = [share(mine, 1, 0, x_peer)]
    along = [share(mine, 0, nz - j, z_peer(j)) for j in range(1, nz)]
    for j in range(1, nz):
        along[j - 1].wait_recv()
        across.append(share(block(x, lax.rem(z + nz - j, nz)), 1, nz - j, x_peer))
    for copy in across:
        copy.wait_recv()
    for copy in list(flying.values()) + parts + along + across:
        copy.wait_send()


def on_device(outer_size, inner_size, queries, key_rows, value_rows):
    count, head = queries.shape
    keys = key_rows.shape[0]
    nz, ny = outer_size // 2, inner_size // 2
    rows = count // 2 // nz
    dma = pltpu.SemaphoreType.DMA
    return pl.pallas_call(
        functools.partial(kernel, outer_size, inner_size),
        out_shape=jax.ShapeDtypeStruct((count, head), jnp.bfloat16),
        in_specs=[pl.BlockSpec(memory_space=pl.ANY)] * 3,
        out_specs=pl.BlockSpec(memory_space=pltpu.VMEM),
        scratch_shapes=[
            pltpu.VMEM((count // 2, head), jnp.bfloat16),
            pltpu.VMEM((2, ny, 2, 2, keys, head), jnp.bfloat16),
            pltpu.VMEM((nz, head, rows), jnp.bfloat16),
            pltpu.VMEM((nz, head, rows), jnp.bfloat16),
            pltpu.VMEM((nz, 8, rows), jnp.float32),
            pltpu.VMEM((nz, 8, rows), jnp.float32),
            dma((3,)),
            dma((2, ny, 2, 2)),
            dma((2, ny, 2, 2)),
            dma((nz, 2)),
            dma((nz, 2)),
            dma((2, nz)),
            dma((2, nz)),
        ],
        compiler_params=pltpu.CompilerParams(
            collective_id=0, has_side_effects=True, vmem_limit_bytes=48 * 1024 * 1024
        ),
        cost_estimate=pl.CostEstimate(
            flops=2 * count * keys * inner_size * head * 2,
            bytes_accessed=2 * (2 * count + 2 * keys) * head,
            transcendentals=count * keys * inner_size,
        ),
    )(queries, key_rows, value_rows)


def solution(mesh):
    return jax.shard_map(
        functools.partial(on_device, mesh.shape["outer"], mesh.shape["inner"]),
        mesh=mesh,
        in_specs=(P("inner", None), P(("outer", "inner"), None), P(("outer", "inner"), None)),
        out_specs=P("inner", None),
        check_vma=False,
    )
```

time: 125 us -> 31.5 us (0.25)
  blocking collectives: 75.7 us -> 0 us
  Pallas kernels: 0 us -> 27.9 us
  between operations: 13.4 us -> 0.01 us
  waiting for transfers between devices: 13.3 us -> 0 us
  other arithmetic: 12.3 us -> 0 us
  matrix products: 7.08 us -> 0 us
  local copies, waits for them, and re-layouts: 2.01 us -> 3.33 us
    all_gather x4 -> x0, blocking collectives: 75.7 us -> none  [the longest x2 62.2 us: merged(): gathered = jax.tree.map(lambda a: lax.all_gather(a, axis), part)]
    pallas_call x0 -> x1, Pallas kernels: none -> 27.9 us  [on_device(): pl.pallas_call(functools.partial(kernel, outer_size, inner_size), out_sha...]
    all_gather x1 -> x0, waiting for transfers between devices: 13.3 us -> none  [merged(): gathered = jax.tree.map(lambda a: lax.all_gather(a, axis), part)]
    add x18 -> x0, other arithmetic: 10.6 us -> none  [the longest x7 10.5 us: combine_partial(): left_sum * left_factor[:, None] + right_sum * right_factor[:, None]]
    dot_general x8 -> x0, matrix products: 7.08 us -> none  [the longest x4 5.03 us: advance(): lax.dot_general(queries, key_tile, (((1,), (1,)), ((), ())), preferred_el...]
    unnamed x2 -> x7, local copies, waits for them, and re-layouts: 0.81 us -> 3.33 us
  transfers between devices with their start and end apart: 1 -> 0, of which waited for: 1 -> 0; matrix products, arithmetic and copies ran while one was open for 0% -> 0% of each run, Pallas kernels for 0% -> 0%
where the time goes in v1:
time: 31.5 us; the launch traced here: 31.3 us
  Pallas kernels  27.9 us (89%)
  local copies, waits for them, and re-layouts  3.33 us (11%)
    pallas_call x1, Pallas kernels, on_device(): pl.pallas_call(functools.partial(kernel, outer_size, inner_size), out_sha...  27.9 us
    unnamed x7, local copies, waits for them, and re-layouts  3.33 us

profile of v1, /device:TPU:0, one launch (start us, length us, event | category | flops | bytes accessed | tf_op | source)
XLA Modules:
  0.0 31.3 jit_solution(15364945321638193723)
XLA Ops:
  0.0 0.0 copy-start
  0.0 0.9 %copy-done = bf16[1024,128]{1,0:T(8,128)(2,1)S(1)} copy-done((bf16[1024,128]{1,0:T(8,128)(2,1)S(1)}, bf16[1024,128]{1,0:T(8,128)(2,1)}, u32[]{:S(2)}) %copy-start) | copy-done | bytes 262168
  1.0 0.0 copy-start.1
  1.0 0.8 %copy-done.1 = bf16[256,128]{1,0:T(8,128)(2,1)S(1)} copy-done((bf16[256,128]{1,0:T(8,128)(2,1)S(1)}, bf16[256,128]{1,0:T(8,128)(2,1)}, u32[]{:S(2)}) %copy-start.1) | copy-done | bytes 65560
  1.8 0.0 copy-start.2
  1.8 0.8 %copy-done.2 = bf16[256,128]{1,0:T(8,128)(2,1)S(1)} copy-done((bf16[256,128]{1,0:T(8,128)(2,1)S(1)}, bf16[256,128]{1,0:T(8,128)(2,1)}, u32[]{:S(2)}) %copy-start.2) | copy-done | bytes 65560
  2.6 27.9 %shard_map.37 = bf16[1024,128]{1,0:T(8,128)(2,1)S(1)} custom-call(bf16[1024,128]{1,0:T(8,128)(2,1)S(1)} %copy-done, bf16[256,128]{1,0:T(8,128)(2,1)S(1)} %copy-done.1, bf16[256,128]{1,0:T(8,128)(2,1)S(1)} %copy-done.2), custom_call_target="tpu_custom_call" | custom-call | flops 536870912 | bytes 655360 | tf_op jit(solution)/shard_map/pallas_call | solution.py:206
  30.5 0.7 %copy.5 = bf16[1024,128]{1,0:T(8,128)(2,1)} copy(bf16[1024,128]{1,0:T(8,128)(2,1)S(1)} %shard_map.37) | data formatting | bytes 524288
Async XLA Ops:
  0.0 0.9 %copy-start = (bf16[1024,128]{1,0:T(8,128)(2,1)S(1)}, bf16[1024,128]{1,0:T(8,128)(2,1)}, u32[]{:S(2)}) copy-start(bf16[1024,128]{1,0:T(8,128)(2,1)} %q_hbm.1) | copy-start | bytes 786436
  1.0 0.8 %copy-start.1 = (bf16[256,128]{1,0:T(8,128)(2,1)S(1)}, bf16[256,128]{1,0:T(8,128)(2,1)}, u32[]{:S(2)}) copy-start(bf16[256,128]{1,0:T(8,128)(2,1)} %k_hbm.1) | copy-start | bytes 196612
  1.8 0.8 %copy-start.2 = (bf16[256,128]{1,0:T(8,128)(2,1)S(1)}, bf16[256,128]{1,0:T(8,128)(2,1)}, u32[]{:S(2)}) copy-start(bf16[256,128]{1,0:T(8,128)(2,1)} %v_hbm.1) | copy-start | bytes 196612

commit v2 on v1

v2 whole, which is shorter than its diff:
```python
import functools
import math

import jax
import jax.numpy as jnp
from jax import lax
from jax.experimental import pallas as pl
from jax.experimental.pallas import tpu as pltpu
from jax.sharding import PartitionSpec as P

MESH = pl.DeviceIdType.MESH
K, V = 0, 1


def kernel(outer_size, inner_size, q_hbm, k_hbm, v_hbm, out_ref, q_vm, kv, sum_ref, peak_ref, total_ref,
           send_acc, recv_acc, send_stat, recv_stat, local_sem, kv_send, kv_recv, z_send, z_recv, g_send, g_recv):
    nz, ny = outer_size // 2, inner_size // 2
    queries, head = out_ref.shape
    half = queries // 2
    rows = half // nz
    outer, inner = lax.axis_index("outer"), lax.axis_index("inner")
    z, x = outer // 2, outer % 2
    y, core = inner // 2, inner % 2

    x_peer = (z * 2 + (1 - x), inner)
    sibling = (outer, y * 2 + (1 - core))
    y_peers = [None] + [(outer, lax.rem(y + j, ny) * 2 + core) for j in range(1, ny)]
    z_peers = [None] + [(lax.rem(z + j, nz) * 2 + x, inner) for j in range(1, nz)]

    def z_peer(j):
        return z_peers[j]

    def slot_of(xr, yr, c):
        chip = (xr if yr == 0 else 1 + yr) if xr == 0 or yr == 0 else ny + yr
        return chip * 2 + c

    local = [
        pltpu.make_async_copy(k_hbm, kv.at[0, K], local_sem.at[0]),
        pltpu.make_async_copy(v_hbm, kv.at[0, V], local_sem.at[1]),
        pltpu.make_async_copy(q_hbm.at[pl.ds(pl.multiple_of(x * half, half), half)], q_vm, local_sem.at[2]),
    ]
    for copy in local:
        copy.start()

    barrier = pltpu.get_barrier_semaphore()
    peers = [x_peer, sibling] + y_peers[1:] + z_peers[1:]
    for peer in peers:
        pl.semaphore_signal(barrier, inc=1, device_id=peer, device_id_type=MESH)
    peak_ref[...] = jnp.full_like(peak_ref, -1e30)
    total_ref[...] = jnp.zeros_like(total_ref)
    sum_ref[...] = jnp.zeros_like(sum_ref)
    local[0].wait()
    local[1].wait()
    pl.semaphore_wait(barrier, len(peers))

    def copy_of(source, slot, which, peer):
        return pltpu.make_async_remote_copy(
            src_ref=kv.at[source, which],
            dst_ref=kv.at[slot, which],
            send_sem=kv_send.at[slot, which],
            recv_sem=kv_recv.at[slot, which],
            device_id=peer,
            device_id_type=MESH,
        )

    def arrive(slot, which):
        copy_of(0, slot, which, sibling).wait_recv()

    def to_sibling(slot, which):
        copy_of(slot, slot + 1, which, sibling).start()

    copy_of(0, slot_of(1, 0, 0), K, x_peer).start()
    for j in range(1, ny):
        copy_of(0, slot_of(0, ny - j, 0), V, y_peers[j]).start()
    to_sibling(0, K)
    to_sibling(0, V)
    copy_of(0, slot_of(1, 0, 0), V, x_peer).start()
    for j in range(1, ny):
        copy_of(0, slot_of(0, ny - j, 0), K, y_peers[j]).start()
    local[2].wait()

    def first_arrivals():
        beside = slot_of(1, 0, 0)
        arrive(beside, K)
        for j in range(1, ny):
            copy_of(beside, slot_of(1, ny - j, 0), K, y_peers[j]).start()
        to_sibling(beside, K)
        for yr in range(ny - 1, 0, -1):
            along = slot_of(0, yr, 0)
            arrive(along, V)
            copy_of(along, slot_of(1, yr, 0), V, x_peer).start()
            to_sibling(along, V)
        arrive(beside, V)
        to_sibling(beside, V)
        for yr in range(ny - 1, 0, -1):
            along = slot_of(0, yr, 0)
            arrive(along, K)
            to_sibling(along, K)

    to_exponent = math.log2(math.e) / math.sqrt(head)

    def step(t, carry):
        pl.when(t == 2)(first_arrivals)
        for yr in range(1, ny):
            @pl.when(t == slot_of(1, yr, 0))
            def _():
                for which in (K, V):
                    arrive(slot_of(1, yr, 0), which)
                    to_sibling(slot_of(1, yr, 0), which)

        @pl.when(t % 2 == 1)
        def _():
            arrive(t, K)
            arrive(t, V)

        scores = lax.dot_general(
            kv[t, K], q_vm[...], (((1,), (1,)), ((), ())), preferred_element_type=jnp.float32
        ) * to_exponent
        peak = jnp.maximum(peak_ref[...], jnp.max(scores, axis=0, keepdims=True))
        factor = jnp.exp2(peak_ref[...] - peak)
        probs = jnp.exp2(scores - peak)
        peak_ref[...] = peak
        total_ref[...] = total_ref[...] * factor + jnp.sum(probs, axis=0, keepdims=True)
        sum_ref[...] = sum_ref[...] * factor + lax.dot_general(
            kv[t, V], probs.astype(jnp.bfloat16), (((0,), (0,)), ((), ())), preferred_element_type=jnp.float32
        )
        return carry

    lax.fori_loop(0, 4 * ny, step, 0)

    weighted, peak, total = sum_ref[...], peak_ref[...], total_ref[...]
    is_peak = lax.broadcasted_iota(jnp.int32, (8, half), 0) < 4
    stat = jnp.where(is_peak, peak, total)
    for zt in range(nz):
        send_acc[zt] = weighted[:, zt * rows:(zt + 1) * rows].astype(jnp.bfloat16)
        send_stat[zt] = stat[:, zt * rows:(zt + 1) * rows]
    parts = []
    for j in range(1, nz):
        target = lax.rem(z + j, nz)
        for at, (src, dst) in enumerate(((send_stat, recv_stat), (send_acc, recv_acc))):
            copy = pltpu.make_async_remote_copy(
                src_ref=src.at[target],
                dst_ref=dst.at[nz - j],
                send_sem=z_send.at[j, at],
                recv_sem=z_recv.at[nz - j, at],
                device_id=z_peer(j),
                device_id_type=MESH,
            )
            copy.start()
            parts.append(copy)
    for copy in parts:
        copy.wait_recv()
    stats = [send_stat[z]] + [recv_stat[s] for s in range(1, nz)]
    sums = [send_acc[z]] + [recv_acc[s] for s in range(1, nz)]
    joint_peak = functools.reduce(jnp.maximum, [s[0:1] for s in stats])
    joint_total = jnp.zeros_like(joint_peak)
    joint_sum = jnp.zeros((head, rows), jnp.float32)
    for s, a in zip(stats, sums):
        factor = jnp.exp2(s[0:1] - joint_peak)
        joint_total = joint_total + s[4:5] * factor
        joint_sum = joint_sum + a.astype(jnp.float32) * factor

    def block(xr, source):
        return out_ref.at[pl.ds(pl.multiple_of((xr * nz + source) * rows, rows), rows)]

    mine = block(x, z)
    mine[...] = (joint_sum / joint_total).T.astype(jnp.bfloat16)

    def share(view, xr, zr, peer):
        copy = pltpu.make_async_remote_copy(
            src_ref=view,
            dst_ref=view,
            send_sem=g_send.at[xr, zr],
            recv_sem=g_recv.at[xr, zr],
            device_id=peer,
            device_id_type=MESH,
        )
        copy.start()
        return copy

    across = [share(mine, 1, 0, x_peer)]
    along = [share(mine, 0, nz - j, z_peer(j)) for j in range(1, nz)]
    for j in range(1, nz):
        along[j - 1].wait_recv()
        across.append(share(block(x, lax.rem(z + nz - j, nz)), 1, nz - j, x_peer))
    for copy in across:
        copy.wait_recv()
    for copy in parts + along + across:
        copy.wait_send()
    for slot in range(1, 4 * ny):
        for which in (K, V):
            copy_of(0, slot, which, sibling).wait_send()


def on_device(outer_size, inner_size, queries, key_rows, value_rows):
    count, head = queries.shape
    keys = key_rows.shape[0]
    nz, ny = outer_size // 2, inner_size // 2
    rows = count // 2 // nz
    dma = pltpu.SemaphoreType.DMA
    return pl.pallas_call(
        functools.partial(kernel, outer_size, inner_size),
        out_shape=jax.ShapeDtypeStruct((count, head), jnp.bfloat16),
        in_specs=[pl.BlockSpec(memory_space=pltpu.HBM)] * 3,
        out_specs=pl.BlockSpec(memory_space=pltpu.VMEM),
        scratch_shapes=[
            pltpu.VMEM((count // 2, head), jnp.bfloat16),
            pltpu.VMEM((4 * ny, 2, keys, head), jnp.bfloat16),
            pltpu.VMEM((head, count // 2), jnp.float32),
            pltpu.VMEM((1, count // 2), jnp.float32),
            pltpu.VMEM((1, count // 2), jnp.float32),
            pltpu.VMEM((nz, head, rows), jnp.bfloat16),
            pltpu.VMEM((nz, head, rows), jnp.bfloat16),
            pltpu.VMEM((nz, 8, rows), jnp.float32),
            pltpu.VMEM((nz, 8, rows), jnp.float32),
            dma((3,)),
            dma((4 * ny, 2)),
            dma((4 * ny, 2)),
            dma((nz, 2)),
            dma((nz, 2)),
            dma((2, nz)),
            dma((2, nz)),
        ],
        compiler_params=pltpu.CompilerParams(
            collective_id=0, has_side_effects=True, vmem_limit_bytes=48 * 1024 * 1024
        ),
        cost_estimate=pl.CostEstimate(
            flops=2 * count * keys * inner_size * head * 2,
            bytes_accessed=2 * (2 * count + 2 * keys) * head,
            transcendentals=count * keys * inner_size,
        ),
    )(*(pltpu.with_memory_space_constraint(a, pltpu.HBM) for a in (queries, key_rows, value_rows)))


def solution(mesh):
    return jax.shard_map(
        functools.partial(on_device, mesh.shape["outer"], mesh.shape["inner"]),
        mesh=mesh,
        in_specs=(P("inner", None), P(("outer", "inner"), None), P(("outer", "inner"), None)),
        out_specs=P("inner", None),
        check_vma=False,
    )
```

time: 31.5 us -> 29.1 us (0.924)
  local copies, waits for them, and re-layouts: 3.33 us -> 0.71 us
    unnamed x7 -> x1, local copies, waits for them, and re-layouts: 3.33 us -> 0.71 us
    pallas_call x1, Pallas kernels: 27.9 us -> 28.2 us  [on_device(): pl.pallas_call(functools.partial(kernel, outer_size, inner_size), out_sha...]
where the time goes in v2:
time: 29.1 us; the launch traced here: 28.9 us
  Pallas kernels  28.2 us (97%)
  local copies, waits for them, and re-layouts  0.71 us (2%)
    pallas_call x1, Pallas kernels, on_device(): pl.pallas_call(functools.partial(kernel, outer_size, inner_size), out_sha...  28.2 us
    unnamed x1, local copies, waits for them, and re-layouts  0.71 us

profile of v2, /device:TPU:0, one launch (start us, length us, event | category | flops | bytes accessed | tf_op | source)
XLA Modules:
  0.0 28.9 jit_solution(5462824645544248300)
XLA Ops:
  0.0 28.2 %shard_map.37 = bf16[1024,128]{1,0:T(8,128)(2,1)S(1)} custom-call(bf16[1024,128]{1,0:T(8,128)(2,1)} %q_hbm.1, bf16[256,128]{1,0:T(8,128)(2,1)} %k_hbm.1, bf16[256,128]{1,0:T(8,128)(2,1)} %v_hbm.1), custom_call_target="tpu_custom_call" | custom-call | flops 536870912 | bytes 655360 | tf_op jit(solution)/shard_map/pallas_call | solution.py:201
  28.2 0.7 %copy.5 = bf16[1024,128]{1,0:T(8,128)(2,1)} copy(bf16[1024,128]{1,0:T(8,128)(2,1)S(1)} %shard_map.37) | data formatting | bytes 524288

commit v3 on v2

--- a/solution.py
+++ b/solution.py
@@ -74,10 +74,15 @@
         copy_of(0, slot_of(0, ny - j, 0), V, y_peers[j]).start()
     to_sibling(0, K)
     to_sibling(0, V)
-    copy_of(0, slot_of(1, 0, 0), V, x_peer).start()
-    for j in range(1, ny):
-        copy_of(0, slot_of(0, ny - j, 0), K, y_peers[j]).start()
     local[2].wait()
+    sent_early = [(slot_of(1, 0, 0), K)] + [(slot_of(0, yr, 0), V) for yr in range(1, ny)]
+
+    def second_sends():
+        for slot, which in sent_early:
+            copy_of(0, slot, which, sibling).wait_send()
+        copy_of(0, slot_of(1, 0, 0), V, x_peer).start()
+        for j in range(1, ny):
+            copy_of(0, slot_of(0, ny - j, 0), K, y_peers[j]).start()
 
     def first_arrivals():
         beside = slot_of(1, 0, 0)
@@ -100,6 +105,7 @@
     to_exponent = math.log2(math.e) / math.sqrt(head)
 
     def step(t, carry):
+        pl.when(t == 1)(second_sends)
         pl.when(t == 2)(first_arrivals)
         for yr in range(1, ny):
             @pl.when(t == slot_of(1, yr, 0))
@@ -160,35 +166,50 @@
         joint_total = joint_total + s[4:5] * factor
         joint_sum = joint_sum + a.astype(jnp.float32) * factor
 
-    def block(xr, source):
-        return out_ref.at[pl.ds(pl.multiple_of((xr * nz + source) * rows, rows), rows)]
-
-    mine = block(x, z)
-    mine[...] = (joint_sum / joint_total).T.astype(jnp.bfloat16)
-
-    def share(view, xr, zr, peer):
-        copy = pltpu.make_async_remote_copy(
-            src_ref=view,
-            dst_ref=view,
-            send_sem=g_send.at[xr, zr],
-            recv_sem=g_recv.at[xr, zr],
+    def block(xs, zs):
+        return out_ref.at[pl.ds(pl.multiple_of((xs * nz + zs) * rows, rows), rows)]
+
+    def share(xr, zs, peer, way):
+        xs = x if way == "z" and xr == 0 or way == "x" and xr == 1 else 1 - x
+        return pltpu.make_async_remote_copy(
+            src_ref=block(xs, zs),
+            dst_ref=block(xs, zs),
+            send_sem=g_send.at[0 if way == "z" else 1, len(shared)],
+            recv_sem=g_recv.at[xr, zs],
             device_id=peer,
             device_id_type=MESH,
         )
+
+    shared = []
+
+    def begin(*args):
+        copy = share(*args)
         copy.start()
-        return copy
-
-    across = [share(mine, 1, 0, x_peer)]
-    along = [share(mine, 0, nz - j, z_peer(j)) for j in range(1, nz)]
-    for j in range(1, nz):
-        along[j - 1].wait_recv()
-        across.append(share(block(x, lax.rem(z + nz - j, nz)), 1, nz - j, x_peer))
-    for copy in across:
-        copy.wait_recv()
-    for copy in parts + along + across:
+        shared.append(copy)
+
+    def landed(xr, zs):
+        share(xr, zs, x_peer, "z").wait_recv()
+
+    block(x, z)[...] = (joint_sum / joint_total).T.astype(jnp.bfloat16)
+    near = z + 1 - 2 * (z % 2)
+    far = [(lax.rem(z // 2 + p, nz // 2) * 2 + b) for p in range(1, nz // 2) for b in range(2)]
+    begin(1, z, x_peer, "x")
+    for zt in far + [near]:
+        begin(0, z, (zt * 2 + x, inner), "z")
+    landed(1, z)
+    begin(1, z, (near * 2 + x, inner), "z")
+    for zs in far:
+        landed(0, zs)
+        begin(1, zs, x_peer, "x")
+    landed(0, near)
+    for zs in [near] + far:
+        landed(1, zs)
+    for copy in parts + shared:
         copy.wait_send()
     for slot in range(1, 4 * ny):
         for which in (K, V):
+            if (slot, which) in sent_early:
+                continue
             copy_of(0, slot, which, sibling).wait_send()
 
 
@@ -218,7 +239,7 @@
             dma((4 * ny, 2)),
             dma((nz, 2)),
             dma((nz, 2)),
-            dma((2, nz)),
+            dma((2, 2 * nz)),
             dma((2, nz)),
         ],
         compiler_params=pltpu.CompilerParams(

time: 29.1 us -> 29.5 us (1.014)
  Pallas kernels: 28.2 us -> 28.7 us
    pallas_call x1, Pallas kernels: 28.2 us -> 28.7 us  [on_device(): pl.pallas_call(functools.partial(kernel, outer_size, inner_size), out_sha...]
where the time goes in v3:
time: 29.5 us; the launch traced here: 29.4 us
  Pallas kernels  28.7 us (97%)
  local copies, waits for them, and re-layouts  0.71 us (2%)
    pallas_call x1, Pallas kernels, on_device(): pl.pallas_call(functools.partial(kernel, outer_size, inner_size), out_sha...  28.7 us
    unnamed x1, local copies, waits for them, and re-layouts  0.71 us

profile of v3, /device:TPU:0, one launch (start us, length us, event | category | flops | bytes accessed | tf_op | source)
XLA Modules:
  0.0 29.4 jit_solution(15780501289901399137)
XLA Ops:
  0.0 28.7 %shard_map.37 = bf16[1024,128]{1,0:T(8,128)(2,1)S(1)} custom-call(bf16[1024,128]{1,0:T(8,128)(2,1)} %q_hbm.1, bf16[256,128]{1,0:T(8,128)(2,1)} %k_hbm.1, bf16[256,128]{1,0:T(8,128)(2,1)} %v_hbm.1), custom_call_target="tpu_custom_call" | custom-call | flops 536870912 | bytes 655360 | tf_op jit(solution)/shard_map/pallas_call | solution.py:222
  28.7 0.7 %copy.5 = bf16[1024,128]{1,0:T(8,128)(2,1)} copy(bf16[1024,128]{1,0:T(8,128)(2,1)S(1)} %shard_map.37) | data formatting | bytes 524288

commit v4 on v3

--- a/solution.py
+++ b/solution.py
@@ -134,76 +134,91 @@
 
     lax.fori_loop(0, 4 * ny, step, 0)
 
-    weighted, peak, total = sum_ref[...], peak_ref[...], total_ref[...]
     is_peak = lax.broadcasted_iota(jnp.int32, (8, half), 0) < 4
-    stat = jnp.where(is_peak, peak, total)
+    stat = jnp.where(is_peak, peak_ref[...], total_ref[...])
     for zt in range(nz):
-        send_acc[zt] = weighted[:, zt * rows:(zt + 1) * rows].astype(jnp.bfloat16)
         send_stat[zt] = stat[:, zt * rows:(zt + 1) * rows]
+        send_acc[zt] = sum_ref[:, zt * rows:(zt + 1) * rows].T.astype(jnp.bfloat16)
+    piece = rows // 2
     parts = []
-    for j in range(1, nz):
+
+    def part_copy(j, at):
         target = lax.rem(z + j, nz)
-        for at, (src, dst) in enumerate(((send_stat, recv_stat), (send_acc, recv_acc))):
-            copy = pltpu.make_async_remote_copy(
-                src_ref=src.at[target],
-                dst_ref=dst.at[nz - j],
-                send_sem=z_send.at[j, at],
-                recv_sem=z_recv.at[nz - j, at],
-                device_id=z_peer(j),
-                device_id_type=MESH,
-            )
+        src, dst = (send_stat, recv_stat) if at == 2 else (send_acc, recv_acc)
+        src, dst = src.at[target], dst.at[nz - j]
+        if at < 2:
+            src, dst = src.at[pl.ds(at * piece, piece)], dst.at[pl.ds(at * piece, piece)]
+        return pltpu.make_async_remote_copy(
+            src_ref=src,
+            dst_ref=dst,
+            send_sem=z_send.at[j, at],
+            recv_sem=z_recv.at[nz - j, at],
+            device_id=z_peer(j),
+            device_id_type=MESH,
+        )
+
+    for at in (2, 0, 1):
+        for j in range(1, nz):
+            copy = part_copy(j, at)
             copy.start()
             parts.append(copy)
-    for copy in parts:
-        copy.wait_recv()
-    stats = [send_stat[z]] + [recv_stat[s] for s in range(1, nz)]
-    sums = [send_acc[z]] + [recv_acc[s] for s in range(1, nz)]
-    joint_peak = functools.reduce(jnp.maximum, [s[0:1] for s in stats])
-    joint_total = jnp.zeros_like(joint_peak)
-    joint_sum = jnp.zeros((head, rows), jnp.float32)
-    for s, a in zip(stats, sums):
-        factor = jnp.exp2(s[0:1] - joint_peak)
-        joint_total = joint_total + s[4:5] * factor
-        joint_sum = joint_sum + a.astype(jnp.float32) * factor
-
-    def block(xs, zs):
-        return out_ref.at[pl.ds(pl.multiple_of((xs * nz + zs) * rows, rows), rows)]
-
-    def share(xr, zs, peer, way):
+
+    def block(xs, zs, at):
+        return out_ref.at[pl.ds(pl.multiple_of((xs * nz + zs) * rows + at * piece, piece), piece)]
+
+    shared = []
+
+    def share(xr, zs, peer, way, at):
         xs = x if way == "z" and xr == 0 or way == "x" and xr == 1 else 1 - x
         return pltpu.make_async_remote_copy(
-            src_ref=block(xs, zs),
-            dst_ref=block(xs, zs),
-            send_sem=g_send.at[0 if way == "z" else 1, len(shared)],
-            recv_sem=g_recv.at[xr, zs],
+            src_ref=block(xs, zs, at),
+            dst_ref=block(xs, zs, at),
+            send_sem=g_send.at[min(len(shared), 4 * nz - 3)],
+            recv_sem=g_recv.at[xr, zs, at],
             device_id=peer,
             device_id_type=MESH,
         )
-
-    shared = []
 
     def begin(*args):
         copy = share(*args)
         copy.start()
         shared.append(copy)
 
-    def landed(xr, zs):
-        share(xr, zs, x_peer, "z").wait_recv()
-
-    block(x, z)[...] = (joint_sum / joint_total).T.astype(jnp.bfloat16)
+    def landed(xr, zs, at):
+        share(xr, zs, x_peer, "z", at).wait_recv()
+
     near = z + 1 - 2 * (z % 2)
     far = [(lax.rem(z // 2 + p, nz // 2) * 2 + b) for p in range(1, nz // 2) for b in range(2)]
-    begin(1, z, x_peer, "x")
-    for zt in far + [near]:
-        begin(0, z, (zt * 2 + x, inner), "z")
-    landed(1, z)
-    begin(1, z, (near * 2 + x, inner), "z")
-    for zs in far:
-        landed(0, zs)
-        begin(1, zs, x_peer, "x")
-    landed(0, near)
-    for zs in [near] + far:
-        landed(1, zs)
+
+    for j in range(1, nz):
+        part_copy(j, 2).wait_recv()
+    stats = [send_stat[z]] + [recv_stat[s] for s in range(1, nz)]
+    joint_peak = functools.reduce(jnp.maximum, [s[0:1] for s in stats])
+    factors = [jnp.exp2(s[0:1] - joint_peak) for s in stats]
+    joint_total = sum(s[4:5] * f for s, f in zip(stats, factors))
+    columns = [jnp.broadcast_to(f, (8, rows)).T[:, 0:1] for f in factors]
+    total_column = jnp.broadcast_to(joint_total, (8, rows)).T[:, 0:1]
+
+    for at in range(2):
+        for j in range(1, nz):
+            part_copy(j, at).wait_recv()
+        span = slice(at * piece, (at + 1) * piece)
+        sums = [send_acc[z, span]] + [recv_acc[s, span] for s in range(1, nz)]
+        joint_sum = sum(a.astype(jnp.float32) * c[span] for a, c in zip(sums, columns))
+        block(x, z, at)[...] = (joint_sum / total_column[span]).astype(jnp.bfloat16)
+        begin(1, z, x_peer, "x", at)
+        for zt in far + [near]:
+            begin(0, z, (zt * 2 + x, inner), "z", at)
+    for at in range(2):
+        landed(1, z, at)
+        begin(1, z, (near * 2 + x, inner), "z", at)
+        for zs in far:
+            landed(0, zs, at)
+            begin(1, zs, x_peer, "x", at)
+    for at in range(2):
+        landed(0, near, at)
+        for zs in [near] + far:
+            landed(1, zs, at)
     for copy in parts + shared:
         copy.wait_send()
     for slot in range(1, 4 * ny):
@@ -230,17 +245,17 @@
             pltpu.VMEM((head, count // 2), jnp.float32),
             pltpu.VMEM((1, count // 2), jnp.float32),
             pltpu.VMEM((1, count // 2), jnp.float32),
-            pltpu.VMEM((nz, head, rows), jnp.bfloat16),
-            pltpu.VMEM((nz, head, rows), jnp.bfloat16),
+            pltpu.VMEM((nz, rows, head), jnp.bfloat16),
+            pltpu.VMEM((nz, rows, head), jnp.bfloat16),
             pltpu.VMEM((nz, 8, rows), jnp.float32),
             pltpu.VMEM((nz, 8, rows), jnp.float32),
             dma((3,)),
             dma((4 * ny, 2)),
             dma((4 * ny, 2)),
-            dma((nz, 2)),
-            dma((nz, 2)),
-            dma((2, 2 * nz)),
-            dma((2, nz)),
+            dma((nz, 3)),
+            dma((nz, 3)),
+            dma((4 * nz - 2,)),
+            dma((2, nz, 2)),
         ],
         compiler_params=pltpu.CompilerParams(
             collective_id=0, has_side_effects=True, vmem_limit_bytes=48 * 1024 * 1024

time: 29.5 us -> 29.2 us (0.990)
  Pallas kernels: 28.7 us -> 28.4 us
    pallas_call x1, Pallas kernels: 28.7 us -> 28.4 us  [on_device(): pl.pallas_call(functools.partial(kernel, outer_size, inner_size), out_sha...]
where the time goes in v4:
time: 29.2 us; the launch traced here: 29.1 us
  Pallas kernels  28.4 us (97%)
  local copies, waits for them, and re-layouts  0.71 us (2%)
    pallas_call x1, Pallas kernels, on_device(): pl.pallas_call(functools.partial(kernel, outer_size, inner_size), out_sha...  28.4 us
    unnamed x1, local copies, waits for them, and re-layouts  0.71 us

profile of v4, /device:TPU:0, one launch (start us, length us, event | category | flops | bytes accessed | tf_op | source)
XLA Modules:
  0.0 29.1 jit_solution(5242988136777370131)
XLA Ops:
  0.0 28.4 %shard_map.37 = bf16[1024,128]{1,0:T(8,128)(2,1)S(1)} custom-call(bf16[1024,128]{1,0:T(8,128)(2,1)} %q_hbm.1, bf16[256,128]{1,0:T(8,128)(2,1)} %k_hbm.1, bf16[256,128]{1,0:T(8,128)(2,1)} %v_hbm.1), custom_call_target="tpu_custom_call" | custom-call | flops 536870912 | bytes 655360 | tf_op jit(solution)/shard_map/pallas_call | solution.py:237
  28.4 0.7 %copy.5 = bf16[1024,128]{1,0:T(8,128)(2,1)} copy(bf16[1024,128]{1,0:T(8,128)(2,1)S(1)} %shard_map.37) | data formatting | bytes 524288

commit v5 on v4

--- a/solution.py
+++ b/solution.py
@@ -12,7 +12,7 @@
 K, V = 0, 1
 
 
-def kernel(outer_size, inner_size, q_hbm, k_hbm, v_hbm, out_ref, q_vm, kv, sum_ref, peak_ref, total_ref,
+def kernel(outer_size, inner_size, q_hbm, k_hbm, v_hbm, out_ref, q_vm, q_turned, kv, sum_ref, peak_ref, total_ref,
            send_acc, recv_acc, send_stat, recv_stat, local_sem, kv_send, kv_recv, z_send, z_recv, g_send, g_recv):
     nz, ny = outer_size // 2, inner_size // 2
     queries, head = out_ref.shape
@@ -75,6 +75,8 @@
     to_sibling(0, K)
     to_sibling(0, V)
     local[2].wait()
+    q_turned[...] = q_vm[...].T
+    tile = math.gcd(half, 128)
     sent_early = [(slot_of(1, 0, 0), K)] + [(slot_of(0, yr, 0), V) for yr in range(1, ny)]
 
     def second_sends():
@@ -119,17 +121,19 @@
             arrive(t, K)
             arrive(t, V)
 
-        scores = lax.dot_general(
-            kv[t, K], q_vm[...], (((1,), (1,)), ((), ())), preferred_element_type=jnp.float32
-        ) * to_exponent
-        peak = jnp.maximum(peak_ref[...], jnp.max(scores, axis=0, keepdims=True))
-        factor = jnp.exp2(peak_ref[...] - peak)
-        probs = jnp.exp2(scores - peak)
-        peak_ref[...] = peak
-        total_ref[...] = total_ref[...] * factor + jnp.sum(probs, axis=0, keepdims=True)
-        sum_ref[...] = sum_ref[...] * factor + lax.dot_general(
-            kv[t, V], probs.astype(jnp.bfloat16), (((0,), (0,)), ((), ())), preferred_element_type=jnp.float32
-        )
+        keys, values = kv[t, K], kv[t, V].T
+        for at in range(0, half, tile):
+            span = slice(at, at + tile)
+            scores = jnp.dot(keys, q_turned[:, span], preferred_element_type=jnp.float32) * to_exponent
+            old_peak = peak_ref[:, span]
+            peak = jnp.maximum(old_peak, jnp.max(scores, axis=0, keepdims=True))
+            factor = jnp.exp2(old_peak - peak)
+            probs = jnp.exp2(scores - peak)
+            peak_ref[:, span] = peak
+            total_ref[:, span] = total_ref[:, span] * factor + jnp.sum(probs, axis=0, keepdims=True)
+            sum_ref[:, span] = sum_ref[:, span] * factor + jnp.dot(
+                values, probs.astype(jnp.bfloat16), preferred_element_type=jnp.float32
+            )
         return carry
 
     lax.fori_loop(0, 4 * ny, step, 0)
@@ -241,6 +245,7 @@
         out_specs=pl.BlockSpec(memory_space=pltpu.VMEM),
         scratch_shapes=[
             pltpu.VMEM((count // 2, head), jnp.bfloat16),
+            pltpu.VMEM((head, count // 2), jnp.bfloat16),
             pltpu.VMEM((4 * ny, 2, keys, head), jnp.bfloat16),
             pltpu.VMEM((head, count // 2), jnp.float32),
             pltpu.VMEM((1, count // 2), jnp.float32),

time: 29.2 us -> 29.1 us (level)
  no operation moved by 1% of the time
where the time goes in v5:
time: 29.1 us; the launch traced here: 29 us
  Pallas kernels  28.3 us (97%)
  local copies, waits for them, and re-layouts  0.71 us (2%)
    pallas_call x1, Pallas kernels, on_device(): pl.pallas_call(functools.partial(kernel, outer_size, inner_size), out_sha...  28.3 us
    unnamed x1, local copies, waits for them, and re-layouts  0.71 us

profile of v5, /device:TPU:0, one launch (start us, length us, event | category | flops | bytes accessed | tf_op | source)
XLA Modules:
  0.0 29.0 jit_solution(4053532702540522555)
XLA Ops:
  0.0 28.3 %shard_map.37 = bf16[1024,128]{1,0:T(8,128)(2,1)S(1)} custom-call(bf16[1024,128]{1,0:T(8,128)(2,1)} %q_hbm.1, bf16[256,128]{1,0:T(8,128)(2,1)} %k_hbm.1, bf16[256,128]{1,0:T(8,128)(2,1)} %v_hbm.1), custom_call_target="tpu_custom_call" | custom-call | flops 536870912 | bytes 655360 | tf_op jit(solution)/shard_map/pallas_call | solution.py:241
  28.3 0.7 %copy.5 = bf16[1024,128]{1,0:T(8,128)(2,1)} copy(bf16[1024,128]{1,0:T(8,128)(2,1)S(1)} %shard_map.37) | data formatting | bytes 524288

commit v6 on v5

--- a/solution.py
+++ b/solution.py
@@ -43,7 +43,8 @@
         copy.start()
 
     barrier = pltpu.get_barrier_semaphore()
-    peers = [x_peer, sibling] + y_peers[1:] + z_peers[1:]
+    corners = [None] + [(z * 2 + (1 - x), lax.rem(y + j, ny) * 2 + core) for j in range(1, ny)]
+    peers = [x_peer, sibling] + y_peers[1:] + corners[1:] + z_peers[1:]
     for peer in peers:
         pl.semaphore_signal(barrier, inc=1, device_id=peer, device_id_type=MESH)
     peak_ref[...] = jnp.full_like(peak_ref, -1e30)
@@ -77,25 +78,20 @@
     local[2].wait()
     q_turned[...] = q_vm[...].T
     tile = math.gcd(half, 128)
-    sent_early = [(slot_of(1, 0, 0), K)] + [(slot_of(0, yr, 0), V) for yr in range(1, ny)]
-
-    def second_sends():
-        for slot, which in sent_early:
-            copy_of(0, slot, which, sibling).wait_send()
-        copy_of(0, slot_of(1, 0, 0), V, x_peer).start()
-        for j in range(1, ny):
-            copy_of(0, slot_of(0, ny - j, 0), K, y_peers[j]).start()
+    copy_of(0, slot_of(1, 0, 0), V, x_peer).start()
+    for j in range(1, ny):
+        copy_of(0, slot_of(0, ny - j, 0), K, y_peers[j]).start()
+    for j in range(1, ny):
+        for which in (K, V):
+            copy_of(0, slot_of(1, ny - j, 0), which, corners[j]).start()
 
     def first_arrivals():
         beside = slot_of(1, 0, 0)
         arrive(beside, K)
-        for j in range(1, ny):
-            copy_of(beside, slot_of(1, ny - j, 0), K, y_peers[j]).start()
         to_sibling(beside, K)
         for yr in range(ny - 1, 0, -1):
             along = slot_of(0, yr, 0)
             arrive(along, V)
-            copy_of(along, slot_of(1, yr, 0), V, x_peer).start()
             to_sibling(along, V)
         arrive(beside, V)
         to_sibling(beside, V)
@@ -107,7 +103,6 @@
     to_exponent = math.log2(math.e) / math.sqrt(head)
 
     def step(t, carry):
-        pl.when(t == 1)(second_sends)
         pl.when(t == 2)(first_arrivals)
         for yr in range(1, ny):
             @pl.when(t == slot_of(1, yr, 0))
@@ -227,8 +222,6 @@
         copy.wait_send()
     for slot in range(1, 4 * ny):
         for which in (K, V):
-            if (slot, which) in sent_early:
-                continue
             copy_of(0, slot, which, sibling).wait_send()
 
 

time: 29.1 us -> 28.7 us (0.986)
  Pallas kernels: 28.3 us -> 27.8 us
    pallas_call x1, Pallas kernels: 28.3 us -> 27.8 us  [on_device(): pl.pallas_call(functools.partial(kernel, outer_size, inner_size), out_sha...]
where the time goes in v6:
time: 28.7 us; the launch traced here: 28.5 us
  Pallas kernels  27.8 us (97%)
  local copies, waits for them, and re-layouts  0.71 us (2%)
    pallas_call x1, Pallas kernels, on_device(): pl.pallas_call(functools.partial(kernel, outer_size, inner_size), out_sha...  27.8 us
    unnamed x1, local copies, waits for them, and re-layouts  0.71 us

profile of v6, /device:TPU:0, one launch (start us, length us, event | category | flops | bytes accessed | tf_op | source)
XLA Modules:
  0.0 28.5 jit_solution(7982322453439919069)
XLA Ops:
  0.0 27.8 %shard_map.37 = bf16[1024,128]{1,0:T(8,128)(2,1)S(1)} custom-call(bf16[1024,128]{1,0:T(8,128)(2,1)} %q_hbm.1, bf16[256,128]{1,0:T(8,128)(2,1)} %k_hbm.1, bf16[256,128]{1,0:T(8,128)(2,1)} %v_hbm.1), custom_call_target="tpu_custom_call" | custom-call | flops 536870912 | bytes 655360 | tf_op jit(solution)/shard_map/pallas_call | solution.py:234
  27.8 0.7 %copy.5 = bf16[1024,128]{1,0:T(8,128)(2,1)} copy(bf16[1024,128]{1,0:T(8,128)(2,1)S(1)} %shard_map.37) | data formatting | bytes 524288

commit v7 on v6

--- a/solution.py
+++ b/solution.py
@@ -45,6 +45,7 @@
     barrier = pltpu.get_barrier_semaphore()
     corners = [None] + [(z * 2 + (1 - x), lax.rem(y + j, ny) * 2 + core) for j in range(1, ny)]
     peers = [x_peer, sibling] + y_peers[1:] + corners[1:] + z_peers[1:]
+    peers += [(lax.rem(z + j, nz) * 2 + (1 - x), inner) for j in range(1, nz)]
     for peer in peers:
         pl.semaphore_signal(barrier, inc=1, device_id=peer, device_id_type=MESH)
     peak_ref[...] = jnp.full_like(peak_ref, -1e30)
@@ -208,15 +209,11 @@
         begin(1, z, x_peer, "x", at)
         for zt in far + [near]:
             begin(0, z, (zt * 2 + x, inner), "z", at)
+            begin(1, z, (zt * 2 + (1 - x), inner), "x", at)
     for at in range(2):
         landed(1, z, at)
-        begin(1, z, (near * 2 + x, inner), "z", at)
-        for zs in far:
+        for zs in [near] + far:
             landed(0, zs, at)
-            begin(1, zs, x_peer, "x", at)
-    for at in range(2):
-        landed(0, near, at)
-        for zs in [near] + far:
             landed(1, zs, at)
     for copy in parts + shared:
         copy.wait_send()

time: 28.7 us -> 28.7 us (level)
  no operation moved by 1% of the time
where the time goes in v7:
time: 28.7 us; the launch traced here: 28.6 us
  Pallas kernels  27.9 us (97%)
  local copies, waits for them, and re-layouts  0.71 us (2%)
    pallas_call x1, Pallas kernels, on_device(): pl.pallas_call(functools.partial(kernel, outer_size, inner_size), out_sha...  27.9 us
    unnamed x1, local copies, waits for them, and re-layouts  0.71 us

profile of v7, /device:TPU:0, one launch (start us, length us, event | category | flops | bytes accessed | tf_op | source)
XLA Modules:
  0.0 28.6 jit_solution(5257890892173581483)
XLA Ops:
  0.0 27.9 %shard_map.37 = bf16[1024,128]{1,0:T(8,128)(2,1)S(1)} custom-call(bf16[1024,128]{1,0:T(8,128)(2,1)} %q_hbm.1, bf16[256,128]{1,0:T(8,128)(2,1)} %k_hbm.1, bf16[256,128]{1,0:T(8,128)(2,1)} %v_hbm.1), custom_call_target="tpu_custom_call" | custom-call | flops 536870912 | bytes 655360 | tf_op jit(solution)/shard_map/pallas_call | solution.py:231
  27.9 0.7 %copy.5 = bf16[1024,128]{1,0:T(8,128)(2,1)} copy(bf16[1024,128]{1,0:T(8,128)(2,1)S(1)} %shard_map.37) | data formatting | bytes 524288
